TPU v7x, 256 devices: a whole 4x4x8 slice. The times are simulated.
256 devices in a mesh: sub: 64 (over x, z, core), dom: 4 (over y).
Axes of the slice: x: 4, y: 4, z: 8, core: 2. Of those that a mesh axis runs over, the one named last changes fastest.
Arguments:
- fine_nodes: bfloat16 [4, 32768, 512], P('dom', 'sub'), may hold values from -6 to 6
- fine_edges: bfloat16 [4, 131072, 512], P('dom', 'sub'), may hold values from -6 to 6
- edge_source: int32 [4, 131072], P('dom', 'sub'), may hold values from 0 to 1023
- edge_target: int32 [4, 131072], P('dom', 'sub'), may hold values from 0 to 511
- edge_blocks: int32 [4, 64], P('dom', 'sub'), may hold values from 1 to 4, as said below
- send_rows: int32 [4, 256, 128], P('dom', 'sub'), may hold values from 0 to 511
- coarse_map: int32 [4, 32768], P('dom', 'sub'), may hold values from 0 to 2047, as said below
- coarse_edges: bfloat16 [4, 16384, 512], P('dom', 'sub'), may hold values from -6 to 6
- coarse_source: int32 [4, 16384], P('dom', 'sub'), may hold values from 0 to 2047
- coarse_target: int32 [4, 16384], P('dom', 'sub'), may hold values from 0 to 31
- edge_first: bfloat16 [2, 1536, 512], replicated, may hold values from -0.15625 to 0.15625
- edge_second: bfloat16 [2, 512, 512], replicated, may hold values from -0.25 to 0.25
- edge_gain: bfloat16 [2, 512], replicated, may hold values from 0.5 to 1.5
- node_first: bfloat16 [2, 1024, 512], replicated, may hold values from -0.1875 to 0.1875
- node_second: bfloat16 [2, 512, 512], replicated, may hold values from -0.25 to 0.25
- node_gain: bfloat16 [2, 512], replicated, may hold values from 0.5 to 1.5
- lift_weight: bfloat16 [512, 512], replicated, may hold values from -0.25 to 0.25
Outputs:
- fine_out: bfloat16 [4, 32768, 512], P('dom', 'sub')
Inputs may be any that keep to these rules, and one draw needn't show every extreme that they name: `edge_blocks`: used blocks of each device; some device uses all 4. `coarse_map`: A fine node held at subdomain s maps to a coarse node held at subdomain s - 1, s or s + 1 of its column.
All inputs are finite; a program needn't handle non-finite values.
Results may differ from a plain program's by a relative error of at most 0.014.
Values may be sent and summed in bfloat16 or wider, within the bound.
A program may use at most 64 MiB of HBM per device.

v0:
```python
import jax
import jax.numpy as jnp
from jax import lax
from jax.sharding import PartitionSpec as P

COARSE_STEPS = 2


EPSILON = 1e-05


def extended(cells, sides, width):
    for axis, dim in sides:
        count = lax.axis_size(axis)
        ends = count - 1
        head = lax.slice_in_dim(cells, 0, width, axis=dim)
        tail = lax.slice_in_dim(cells, cells.shape[dim] - width, cells.shape[dim], axis=dim)
        cells = jnp.concatenate(
            [
                lax.ppermute(tail, axis, [(i, (i + 1) % count) for i in range(ends)]),
                cells,
                lax.ppermute(head, axis, [((i + 1) % count, i) for i in range(ends)]),
            ],
            axis=dim,
        )
    return cells


def layer_norm(values, scaling):
    centre = values - jnp.mean(values, axis=-1, keepdims=True)
    variance = jnp.mean(centre * centre, axis=-1, keepdims=True)
    return centre * lax.rsqrt(variance + EPSILON) * scaling.astype(jnp.float32)


def two_layer(pieces, weight_in, weight_out, scaling):
    breadth = pieces[0].shape[1]
    running = jnp.dot(pieces[0], weight_in[:breadth], preferred_element_type=jnp.float32)
    for number, member in enumerate(pieces[1:]):
        starting = (number + 1) * breadth
        running = running + jnp.dot(
            member, weight_in[starting : starting + breadth], preferred_element_type=jnp.float32
        )
    hidden = jax.nn.silu(running).astype(jnp.bfloat16)
    return layer_norm(jnp.dot(hidden, weight_out, preferred_element_type=jnp.float32), scaling)


def edge_message(latents, from_source, from_target, layer_index, weights):
    message = two_layer(
        (latents, from_source, from_target),
        weights[0][layer_index],
        weights[1][layer_index],
        weights[2][layer_index],
    )
    return (latents.astype(jnp.float32) + message).astype(jnp.bfloat16)


def node_refresh(states, summed, layer_index, weights):
    update = two_layer(
        (states, summed.astype(jnp.bfloat16)),
        weights[3][layer_index],
        weights[4][layer_index],
        weights[5][layer_index],
    )
    return (states.astype(jnp.float32) + update).astype(jnp.bfloat16)


def one_hot_rows(count_rows, labels):
    return (jnp.arange(count_rows, dtype=jnp.int32)[:, None] == labels[None, :]).astype(
        jnp.bfloat16
    )


def collect(coarse_own):
    return lax.all_gather(coarse_own, "sub", axis=0, tiled=True)


def per_device(
    fine_nodes,
    fine_edges,
    edge_source,
    edge_target,
    edge_blocks,
    send_rows,
    coarse_map,
    coarse_edges,
    coarse_source,
    coarse_target,
    edge_first,
    edge_second,
    edge_gain,
    node_first,
    node_second,
    node_gain,
    lift_weight,
):
    weights = (edge_first, edge_second, edge_gain, node_first, node_second, node_gain)
    states = fine_nodes[0]
    node_count = states.shape[0]
    breadth = states.shape[1]
    coarse_rows = node_count // 16
    sub_index = lax.axis_index("sub")
    picked = states[send_rows[0]]
    along_sub = extended(picked[0:2], (("sub", 0),), 1)
    along_dom = extended(picked[2:4], (("dom", 0),), 1)
    lookup = jnp.concatenate(
        [states, along_sub[0], along_sub[3], along_dom[0], along_dom[3]], axis=0
    )
    latents = fine_edges[0]
    sources = edge_source[0]
    targets = edge_target[0]

    def edge_block(number, summed):
        starting = number * node_count
        block_latents = lax.dynamic_slice_in_dim(latents, starting, node_count, 0)
        block_sources = lax.dynamic_slice_in_dim(sources, starting, node_count, 0)
        block_targets = lax.dynamic_slice_in_dim(targets, starting, node_count, 0)
        renewed = edge_message(
            block_latents, lookup[block_sources], states[block_targets], 0, weights
        )
        return summed + jnp.dot(
            one_hot_rows(node_count, block_targets), renewed, preferred_element_type=jnp.float32
        )

    summed = lax.fori_loop(
        0, edge_blocks[0, 0], edge_block, jnp.zeros((node_count, breadth), jnp.float32)
    )
    refined = node_refresh(states, summed, 0, weights)
    mapped = coarse_map[0]
    local_slots = mapped - (sub_index - 1) * coarse_rows
    partial_rows = jnp.dot(
        one_hot_rows(3 * coarse_rows, local_slots), refined, preferred_element_type=jnp.float32
    )
    padded = extended(
        partial_rows.reshape(3, coarse_rows, breadth).astype(jnp.bfloat16), (("sub", 0),), 1
    ).astype(jnp.float32)
    coarse_own = (0.25 * (padded[0] + padded[2] + padded[4])).astype(jnp.bfloat16)
    column = collect(coarse_own)
    coarse_latents = coarse_edges[0]
    coarse_from = coarse_source[0]
    coarse_to = coarse_target[0]
    for repeat in range(COARSE_STEPS):
        if repeat > 0:
            column = collect(coarse_own)
        coarse_latents = edge_message(
            coarse_latents, column[coarse_from], coarse_own[coarse_to], 1, weights
        )
        summed_coarse = jnp.dot(
            one_hot_rows(coarse_rows, coarse_to), coarse_latents, preferred_element_type=jnp.float32
        )
        coarse_own = node_refresh(coarse_own, summed_coarse, 1, weights)
    beside_all = extended(coarse_own, (("sub", 0),), coarse_rows)
    lifted = beside_all[mapped - (sub_index - 1) * coarse_rows]
    output = (
        refined.astype(jnp.float32)
        + jnp.dot(lifted, lift_weight, preferred_element_type=jnp.float32)
    ).astype(jnp.bfloat16)
    return output[None]


def solution(mesh):
    placed = (
        P("dom", "sub", None),
        P("dom", "sub", None),
        P("dom", "sub"),
        P("dom", "sub"),
        P("dom", "sub"),
        P("dom", "sub", None),
        P("dom", "sub"),
        P("dom", "sub", None),
        P("dom", "sub"),
        P("dom", "sub"),
        P(),
        P(),
        P(),
        P(),
        P(),
        P(),
        P(),
    )
    return jax.shard_map(
        per_device, mesh=mesh, in_specs=placed, out_specs=P("dom", "sub", None), check_vma=False
    )
```

profile of v0, /device:TPU:16, one launch (start us, length us, event | category | flops | bytes accessed | tf_op | source)
XLA Modules:
  0.0 303.0 jit_solution(13882590554191685380)
XLA Ops:
  6.5 0.7 fusion.104
  7.3 3.1 %gather_fusion.2 = bf16[512,512]{1,0:T(8,128)(2,1)S(1)} fusion(bf16[512,512]{1,0:T(8,128)(2,1)} %bitcast.177, s32[1024]{0:T(1024)S(1)} %pad_clamp_fusion.5), kind=kCustom, calls=%fused_computation.2 | custom fusion | bytes 1050624 | tf_op jit(solution)/shard_map/gather | solution.py:102
  10.6 2.4 collective-permute-start
  13.1 1.3 collective-permute-start.1
  14.5 3.2 %collective-permute-start.2 = (bf16[1,128,512]{1,2,0:T(8,128)(2,1)S(1)}, bf16[1,128,512]{1,2,0:T(8,128)(2,1)S(1)}, u32[]{:S(2)}, u32[]{:S(2)}) collective-permute-start(bf16[1,128,512]{1,2,0:T(8,128)(2,1)S(1)} %bitcast.184), channel_id=1, source_target_pairs={{0,1},{1,2},{2,3},{4,5},{5,6},{6,7},{8,9},{9,10},{10,11},{12,13},{... | collective-permute-start | bytes 393224 | tf_op jit(solution)/shard_map/ppermute | solution.py:20
  17.8 2.7 collective-permute-start.3
  20.8 4.1 %copy.30 = bf16[1,2048,512]{1,2,0:T(8,128)(2,1)} copy(bf16[1,2048,512]{2,1,0:T(8,128)(2,1)} %param.20) | data formatting | bytes 4194304 | tf_op args[1]
  24.9 2.5 fusion.50
  27.4 0.6 compare_select_fusion.2
  28.0 0.9 bitcast_dynamic-update-slice_fusion.4
  29.2 0.5 copy.36
  29.7 1.1 broadcast_in_dim.8
  30.8 17.5 %while.10 = (s32[]{:T(128)}, f32[512,512]{1,0:T(8,128)}, s32[]{:T(128)}, s32[2048]{0:T(1024)}, bf16[2048,512]{0,1:T(8,128)(2,1)}, /*index=5*/bf16[2,1536,512]{2,...) while((s32[]{:T(128)}, f32[512,512]{1,0:T(8,128)}, ...), condition=%wide.region_3.4_spmd, body=%wide.region_0.3_spmd.sunk | while | flops 1347164160 | bytes 15781063 | solution.py:124
  31.5 1.7 fusion.155
  33.2 0.8 compare_select_fusion.7
  34.0 2.6 gather_fusion
  36.6 2.6 convolution_add_fusion.13
  39.2 2.6 gather_fusion.1
  41.8 2.7 fusion.156
  44.7 3.0 convolution_add_fusion.14
  48.4 2.9 fusion.114
  52.1 3.5 %collective-permute-start.4 = (bf16[1,32,512]{2,1,0:T(8,128)(2,1)S(1)}, bf16[1,32,512]{2,1,0:T(8,128)(2,1)S(1)}, u32[]{:S(2)}, u32[]{:S(2)}) collective-permute-start(bf16[1,32,512]{2,1,0:T(8,128)(2,1)S(1)} %get-tuple-element.119), channel_id=1, source_target_pairs={{0,4},{4,8},{8,12},{12,16},{16,20},{20,24},{24,28},{28,32},{32,36}... | collective-permute-start | bytes 98312 | tf_op jit(solution)/shard_map/ppermute | solution.py:20
  55.6 1.3 collective-permute-start.5
  56.9 3.6 %collective-permute-done.5 = bf16[1,32,512]{2,1,0:T(8,128)(2,1)S(1)} collective-permute-done((bf16[1,32,512]{2,1,0:T(8,128)(2,1)S(1)}, bf16[1,32,512]{2,1,0:T(8,128)(2,1)S(1)}, u32[]{:S(2)}, u32[]{:S(2)}) %collective-permute-start.5) | collective-permute-done | bytes 32800 | tf_op jit(solution)/shard_map/ppermute | solution.py:22
  60.5 0.6 fusion.95
  61.5 1.3 fusion.41
  62.8 1.2 gather_fusion.4
  64.0 1.2 fusion.45
  65.2 128.0 %all-gather.6.cloned.1.call-done = bf16[1,2048,512]{2,1,0:T(8,128)(2,1)} async-done(((bf16[1,32,512]{2,1,0:T(8,128)(2,1)}), bf16[1,2048,512]{2,1,0:T(8,128)(2,1)}) %all-gather.6.cloned.1.call-update) | async-done | bytes 2097168 | tf_op jit(solution)/shard_map/all_gather | solution.py:74
  193.2 3.1 %gather_fusion.3 = bf16[256,512]{1,0:T(8,128)(2,1)S(1)} fusion(bf16[2048,512]{1,0:T(8,128)(2,1)} %bitcast.181, s32[1024]{0:T(1024)S(1)} %pad_clamp_fusion.4), kind=kCustom, calls=%fused_computation.3 | custom fusion | bytes 525312 | tf_op jit(solution)/shard_map/gather | solution.py:145
  196.3 1.3 convolution_add_fusion.8
  197.6 1.9 fusion.119
  199.9 1.5 multiply_convert_fusion.5
  201.9 0.7 add_convert_fusion.10
  202.7 2.0 gather_fusion.6
  204.7 1.2 fusion.43
  205.9 1.3 fusion.39
  207.3 70.5 %all-gather.4.cloned.1.call-done = bf16[2048,512]{1,0:T(8,128)(2,1)} async-done(((bf16[32,512]{1,0:T(8,128)(2,1)}), bf16[2048,512]{1,0:T(8,128)(2,1)}) %all-gather.4.cloned.1.call-update) | async-done | bytes 2097168 | tf_op jit(solution)/shard_map/all_gather | solution.py:74
  277.8 3.1 %gather_fusion.5 = bf16[256,512]{1,0:T(8,128)(2,1)S(1)} fusion(bf16[2048,512]{1,0:T(8,128)(2,1)} %all-gather.4.cloned.1.call-done, s32[1024]{0:T(1024)S(1)} %pad_clamp_fusion.4), kind=kCustom, calls=%fused_computation.5 | custom fusion | bytes 525312 | tf_op jit(solution)/shard_map/gather | solution.py:145
  280.8 2.1 convolution_add_fusion.6
  283.0 2.1 fusion.123
  285.3 1.5 multiply_convert_fusion.4
  287.4 2.2 collective-permute-start.6
  289.6 1.3 collective-permute-start.7
  290.9 1.8 collective-permute-done.7
  292.7 2.0 gather_fusion.7
  294.7 0.5 fusion.23
  295.2 1.0 copy.39
  (91 shorter events, 3.9 us)
Async XLA Ops:
  6.5 288.2 %copy-start = (bf16[512,512]{1,0:T(8,128)(2,1)S(1)}, bf16[512,512]{1,0:T(8,128)(2,1)}, u32[]{:S(2)}) copy-start(bf16[512,512]{1,0:T(8,128)(2,1)} %param.35) | copy-start | bytes 1572868
  6.5 186.6 %all-gather.6.cloned.1.call-start = ((), (), s32[]{:S(2)}) async-start(), calls=%async_computation.1 | async-start | bytes 2129920 | tf_op jit(solution)/shard_map/all_gather | solution.py:74
  10.4 10.1 %copy-start.1 = (bf16[1,512,512]{2,1,0:T(8,128)(2,1)S(1)}, bf16[1,512,512]{2,1,0:T(8,128)(2,1)}, u32[]{:S(2)}) copy-start(bf16[1,512,512]{2,1,0:T(8,128)(2,1)} %param.19) | copy-start | bytes 1572868
  10.6 17.5 %collective-permute-start = (bf16[1,128,512]{1,2,0:T(8,128)(2,1)S(1)}, bf16[1,128,512]{1,2,0:T(8,128)(2,1)}, u32[]{:S(2)}, u32[]{:S(2)}) collective-permute-start(bf16[1,128,512]{1,2,0:T(8,128)(2,1)S(1)} %bitcast.187), channel_id=1, source_target_pairs={{0,4},{4,8},{8,12},{12,16},{16,20},{20,24},{24,28},{28,32},{32,36}... | collective-permute-start | bytes 393224 | tf_op jit(solution)/shard_map/ppermute | solution.py:20
  13.1 15.9 %collective-permute-start.1 = (bf16[1,128,512]{1,2,0:T(8,128)(2,1)S(1)}, bf16[1,128,512]{1,2,0:T(8,128)(2,1)S(1)}, u32[]{:S(2)}, u32[]{:S(2)}) collective-permute-start(bf16[1,128,512]{1,2,0:T(8,128)(2,1)S(1)} %bitcast.186), channel_id=1, source_target_pairs={{4,0},{8,4},{12,8},{16,12},{20,16},{24,20},{28,24},{32,28},{36,32}... | collective-permute-start | bytes 393224 | tf_op jit(solution)/shard_map/ppermute | solution.py:22
  14.5 14.5 %collective-permute-start.2 = (bf16[1,128,512]{1,2,0:T(8,128)(2,1)S(1)}, bf16[1,128,512]{1,2,0:T(8,128)(2,1)S(1)}, u32[]{:S(2)}, u32[]{:S(2)}) collective-permute-start(bf16[1,128,512]{1,2,0:T(8,128)(2,1)S(1)} %bitcast.184), channel_id=1, source_target_pairs={{0,1},{1,2},{2,3},{4,5},{5,6},{6,7},{8,9},{9,10},{10,11},{12,13},{... | collective-permute-start | bytes 393224 | tf_op jit(solution)/shard_map/ppermute | solution.py:20
  17.8 11.3 %collective-permute-start.3 = (bf16[1,128,512]{1,2,0:T(8,128)(2,1)S(1)}, bf16[1,128,512]{1,2,0:T(8,128)(2,1)S(1)}, u32[]{:S(2)}, u32[]{:S(2)}) collective-permute-start(bf16[1,128,512]{1,2,0:T(8,128)(2,1)S(1)} %bitcast.185), channel_id=1, source_target_pairs={{1,0},{2,1},{3,2},{5,4},{6,5},{7,6},{9,8},{10,9},{11,10},{13,12},{... | collective-permute-start | bytes 393224 | tf_op jit(solution)/shard_map/ppermute | solution.py:22
  20.7 4.2 %copy-start.4 = (bf16[1,512,512]{1,2,0:T(8,128)(2,1)}, bf16[1,512,512]{1,2,0:T(8,128)(2,1)S(1)}, u32[]{:S(2)}) copy-start(bf16[1,512,512]{1,2,0:T(8,128)(2,1)S(1)} %copy.29) | copy-start | bytes 1572868
  24.9 2.5 copy-start.12
  24.9 2.5 copy-start.13
  28.0 2.8 copy-start.10
  48.4 3.1 %copy-start.5 = (bf16[1,512,512]{1,2,0:T(8,128)(2,1)S(1)}, bf16[1,512,512]{1,2,0:T(8,128)(2,1)}, u32[]{:S(2)}) copy-start(bf16[1,512,512]{1,2,0:T(8,128)(2,1)} %copy-done.4) | copy-start | bytes 1572868
  51.3 10.1 %copy-start.14 = (s32[1,256]{1,0:T(1,128)S(1)}, s32[1,256]{1,0:T(1,128)}, u32[]{:S(2)}) copy-start(s32[1,256]{1,0:T(1,128)} %param.27) | copy-start | bytes 3076
  51.3 10.1 %copy-start.15 = (s32[1,256]{1,0:T(1,128)S(1)}, s32[1,256]{1,0:T(1,128)}, u32[]{:S(2)}) copy-start(s32[1,256]{1,0:T(1,128)} %param.28) | copy-start | bytes 3076
  51.3 10.2 %copy-start.7 = (bf16[1,256,512]{2,1,0:T(8,128)(2,1)S(1)}, bf16[1,256,512]{2,1,0:T(8,128)(2,1)}, u32[]{:S(2)}) copy-start(bf16[1,256,512]{2,1,0:T(8,128)(2,1)} %param.26) | copy-start | bytes 786436
  52.1 4.8 %collective-permute-start.4 = (bf16[1,32,512]{2,1,0:T(8,128)(2,1)S(1)}, bf16[1,32,512]{2,1,0:T(8,128)(2,1)S(1)}, u32[]{:S(2)}, u32[]{:S(2)}) collective-permute-start(bf16[1,32,512]{2,1,0:T(8,128)(2,1)S(1)} %get-tuple-element.119), channel_id=1, source_target_pairs={{0,4},{4,8},{8,12},{12,16},{16,20},{20,24},{24,28},{28,32},{32,36}... | collective-permute-start | bytes 98312 | tf_op jit(solution)/shard_map/ppermute | solution.py:20
  55.6 4.9 %collective-permute-start.5 = (bf16[1,32,512]{2,1,0:T(8,128)(2,1)S(1)}, bf16[1,32,512]{2,1,0:T(8,128)(2,1)S(1)}, u32[]{:S(2)}, u32[]{:S(2)}) collective-permute-start(bf16[1,32,512]{2,1,0:T(8,128)(2,1)S(1)} %get-tuple-element.120), channel_id=1, source_target_pairs={{4,0},{8,4},{12,8},{16,12},{20,16},{24,20},{28,24},{32,28},{36,32}... | collective-permute-start | bytes 98312 | tf_op jit(solution)/shard_map/ppermute | solution.py:22
  61.1 1.7 copy-start.2
  61.2 216.6 %all-gather.4.cloned.1.call-start = ((), (), s32[]{:S(2)}) async-start(), calls=%async_computation | async-start | bytes 2129920 | tf_op jit(solution)/shard_map/all_gather | solution.py:74
  197.6 2.3 copy-start.16
  199.5 1.9 copy-start.6
  199.9 6.0 %copy-start.8 = (bf16[256,512]{1,0:T(8,128)(2,1)}, bf16[256,512]{1,0:T(8,128)(2,1)S(1)}, u32[]{:S(2)}) copy-start(bf16[256,512]{1,0:T(8,128)(2,1)S(1)} %add_convert_fusion.4) | copy-start | bytes 786436
  202.6 2.1 copy-start.3
  283.0 2.3 copy-start.9
  285.0 5.9 %copy-start.11 = (s32[512,1]{0,1:T(1,128)S(1)}, s32[512,1]{0,1:T(1,128)}, u32[]{:S(2)}) copy-start(s32[512,1]{0,1:T(1,128)} %get-tuple-element.110) | copy-start | bytes 6148
  287.4 3.5 %collective-permute-start.6 = (bf16[32,512]{1,0:T(8,128)(2,1)S(1)}, bf16[32,512]{1,0:T(8,128)(2,1)S(1)}, u32[]{:S(2)}, u32[]{:S(2)}) collective-permute-start(bf16[32,512]{1,0:T(8,128)(2,1)S(1)} %add_convert_fusion.7), channel_id=1, source_target_pairs={{0,4},{4,8},{8,12},{12,16},{16,20},{20,24},{24,28},{28,32},{32,36}... | collective-permute-start | bytes 98312 | tf_op jit(solution)/shard_map/ppermute | solution.py:20
  289.6 3.1 %collective-permute-start.7 = (bf16[32,512]{1,0:T(8,128)(2,1)S(1)}, bf16[32,512]{1,0:T(8,128)(2,1)S(1)}, u32[]{:S(2)}, u32[]{:S(2)}) collective-permute-start(bf16[32,512]{1,0:T(8,128)(2,1)S(1)} %add_convert_fusion.7), channel_id=1, source_target_pairs={{4,0},{8,4},{12,8},{16,12},{20,16},{24,20},{28,24},{32,28},{36,32}... | collective-permute-start | bytes 98312 | tf_op jit(solution)/shard_map/ppermute | solution.py:22
Sparse Core Ops, SparseCore 0:
  61.3 131.8 all-gather.5
  202.8 74.9 all-gather.3
where the time goes:
time: 308 us; the launch traced here: 303 us
  waiting for transfers between devices  204 us (66%)
  matrix products  32.2 us (10%)
  local copies, waits for them, and re-layouts  28.3 us (9%)
  starting transfers between devices  18 us (6%)
  between operations  14 us (5%)
  other arithmetic  5.2 us (2%)
    all_gather x2, waiting for transfers between devices, collect(): return lax.all_gather(coarse_own, 'sub', axis=0, tiled=True)  198 us
    ppermute x4, starting transfers between devices, extended(): lax.ppermute(tail, axis, [(i, (i + 1) % count) for i in range(ends)])  11.3 us
    dot_general x6, matrix products, two_layer(): jnp.dot(hidden, weight_out, preferred_element_type=jnp.float32)  10.1 us
    dot_general x6, matrix products, two_layer(): jnp.dot(pieces[0], weight_in[:breadth], preferred_element_type=jnp.float32)  9.3 us
    dot_general x5, matrix products, two_layer(): jnp.dot(member, weight_in[starting:starting + breadth], preferred_element...  9.07 us
    ppermute x4, starting transfers between devices, extended(): lax.ppermute(head, axis, [((i + 1) % count, i) for i in range(ends)])  6.53 us
  transfers between devices with their start and end apart: 10, of which 4 were waited for; matrix products, arithmetic and copies ran while one was open for 6% of the time, Pallas kernels for 0%

commit v1 on v0

v1 whole, which is shorter than its diff:
```python
import functools

import jax
import jax.numpy as jnp
from jax import lax
from jax.experimental import pallas as pl
from jax.experimental.pallas import tpu as pltpu
from jax.sharding import PartitionSpec as P

EPSILON = 1e-05
BF = jnp.bfloat16
F32 = jnp.float32
MESH = pl.DeviceIdType.MESH
ORDER = (0, -1, 1, -2, 2, -3, 3, -4)
NX, NZ = 4, 8
GROUPS = ((0, 1), (1, 5), (5, 8))


def dot(a, b):
    return jnp.dot(a, b, preferred_element_type=F32)


def silu(v):
    return 0.5 * v * (1.0 + jnp.tanh(0.5 * v))


def layer_norm(v, gain):
    centre = v - jnp.mean(v, axis=-1, keepdims=True)
    variance = jnp.mean(centre * centre, axis=-1, keepdims=True)
    return centre * lax.rsqrt(variance + EPSILON) * gain


def column_of(row):
    n = row.shape[1]
    parts = [
        jnp.transpose(jnp.broadcast_to(row[:, i : i + 128], (128, 128))) for i in range(0, n, 128)
    ]
    return parts[0] if len(parts) == 1 else jnp.concatenate(parts, axis=0)


def ones_where(mask):
    return jnp.where(mask, 1.0, 0.0).astype(BF)


def pick_matrix(col, lanes, offset=0):
    reps = lanes // 128
    wide = col if reps == 1 else jnp.concatenate([col] * reps, axis=1)
    return ones_where(wide == lax.broadcasted_iota(jnp.int32, wide.shape, 1) + offset)


def sum_matrix(row, rows):
    shape = (rows, row.shape[1])
    return ones_where(jnp.broadcast_to(row, shape) == lax.broadcasted_iota(jnp.int32, shape, 0))


def kernel(
    fn, fe, es, et, eb, sr, cm, ce, cs, ct, ef, e2, eg, nf, n2, ng, lw,
    out,
    states, lat, wef, we2, wnf, wn2, wlw, cev,
    a_own, b_tgt, pick, halo, pre, src_col, tgt_col, agg, node_pre, refined,
    part, part_in, col0, col1, choice, choice_in, own, csrc, cs_other, sb, outv,
    load_sem, out_sem, halo_ss, halo_rs, part_ss, part_rs, ag_ss, ag_rs, set_ss, set_rs,
):
    s = lax.axis_index("sub")
    d = lax.axis_index("dom")
    subs = NX * NZ * 2
    x = s // (2 * NZ)
    z = lax.rem(s // 2, NZ)
    c = lax.rem(s, 2)
    s_up, s_down = lax.rem(s + 1, subs), lax.rem(s + subs - 1, subs)
    d_up, d_down = lax.rem(d + 1, 4), lax.rem(d + 3, 4)

    def place(xx, zz, cc):
        return xx * (2 * NZ) + zz * 2 + cc

    xs = [lax.rem(x + k, NX) for k in range(NX)]
    dev_z = {k: place(x, lax.rem(z + k + NZ, NZ), c) for k in (1, -1, 2, -2)}
    dev_x = [place(xs[k], z, c) for k in range(NX)]
    sibling = place(x, z, 1 - c)

    barrier = pltpu.get_barrier_semaphore()
    for partner in (s_up, s_down, *dev_z.values(), dev_x[1], dev_x[2], dev_x[3]):
        pl.semaphore_signal(barrier, inc=1, device_id={"sub": partner}, device_id_type=MESH)
    for partner in (d_up, d_down):
        pl.semaphore_signal(barrier, inc=1, device_id={"dom": partner}, device_id_type=MESH)

    pairs = [
        (fn.at[0], states),
        (ef.at[0], wef.at[0]),
        (fe.at[0], lat),
        (e2, we2),
        (nf.at[0], wnf.at[0]),
        (n2, wn2),
        (ce.at[0], cev),
        (ef.at[1], wef.at[1]),
        (nf.at[1], wnf.at[1]),
        (lw, wlw),
    ]
    loads = [pltpu.make_async_copy(a, b, load_sem.at[i]) for i, (a, b) in enumerate(pairs)]
    for copy in loads:
        copy.start()

    w = states.shape[1]
    nodes = states.shape[0]
    halo_rows = halo.shape[1]
    coarse = own.shape[0]
    c_edges = cev.shape[0]

    def remote(src, dst, ss, rs, sub=None, dom=None):
        device = {"sub": sub} if dom is None else {"dom": dom}
        return pltpu.make_async_remote_copy(
            src_ref=src, dst_ref=dst, send_sem=ss, recv_sem=rs,
            device_id=device, device_id_type=MESH,
        )

    loads[0].wait()
    loads[1].wait()
    a_own[...] = dot(states[...], wef[0, w : 2 * w]).astype(BF)
    listed = jnp.concatenate([column_of(sr[0, k : k + 1, :]) for k in range(4)], axis=0)
    picked = dot(pick_matrix(listed, nodes), a_own[...]).astype(BF)
    pick[...] = picked.reshape(4, halo_rows, w)
    pl.semaphore_wait(barrier, 11)
    halo_copies = [
        remote(pick.at[1], halo.at[0], halo_ss.at[0], halo_rs.at[0], sub=s_up),
        remote(pick.at[0], halo.at[1], halo_ss.at[1], halo_rs.at[1], sub=s_down),
        remote(pick.at[3], halo.at[2], halo_ss.at[2], halo_rs.at[2], dom=d_up),
        remote(pick.at[2], halo.at[3], halo_ss.at[3], halo_rs.at[3], dom=d_down),
    ]
    for copy in halo_copies:
        copy.start()
    cs_copy = remote(cs, cs_other, ag_ss.at[0, 21], ag_rs.at[0, 21], sub=sibling)
    cs_copy.start()

    b_tgt[...] = dot(states[...], wef[0, 2 * w : 3 * w]).astype(BF)
    edges = lat.shape[0]
    src_col[...] = column_of(es[...])
    tgt_col[...] = column_of(et[...])
    loads[2].wait()
    blocks = edges // nodes

    def first(b, carry):
        here = pl.ds(pl.multiple_of(b * nodes, nodes), nodes)
        pre[here, :] = (
            dot(lat[here, :], wef[0, 0:w])
            + dot(pick_matrix(src_col[here, :], nodes), a_own[...])
            + dot(pick_matrix(tgt_col[here, :], nodes), b_tgt[...])
        )
        return carry

    lax.fori_loop(0, blocks, first, 0)
    loads[4].wait()
    node_pre[...] = dot(states[...], wnf[0, 0:w])
    loads[3].wait()

    for copy in halo_copies:
        copy.wait()
    exists = (s > 0, s < subs - 1, d > 0, d < 3)
    for k in range(4):
        halo[k] = jnp.where(exists[k], halo[k].astype(F32), 0.0).astype(BF)
    agg[...] = jnp.zeros_like(agg)
    edge_gain = eg[...].astype(F32)
    node_gain = ng[...].astype(F32)
    used = eb[...]

    def second(b, carry):
        start = pl.multiple_of(b * nodes, nodes)
        here = pl.ds(start, nodes)
        table = halo[...].reshape(4 * halo_rows, w)
        v = pre[here, :] + dot(pick_matrix(src_col[here, :], 4 * halo_rows, nodes), table)
        message = layer_norm(dot(silu(v).astype(BF), we2[0]), edge_gain[0:1])
        renewed = (lat[here, :].astype(F32) + message).astype(BF)
        targets = jnp.where(b < used, et[:, here], -1)
        agg[...] += dot(sum_matrix(targets, nodes), renewed)
        return carry

    lax.fori_loop(0, blocks, second, 0)

    loads[5].wait()
    v = node_pre[...] + dot(agg[...].astype(BF), wnf[0, w : 2 * w])
    update = layer_norm(dot(silu(v).astype(BF), wn2[0]), node_gain[0:1])
    refined[...] = (states[...].astype(F32) + update).astype(BF)
    slots = cm[...] - (s - 1) * coarse
    partial = dot(sum_matrix(slots, 3 * coarse), refined[...])
    part[0] = partial[0:coarse].astype(BF)
    part[1] = partial[2 * coarse : 3 * coarse].astype(BF)
    part_copies = [
        remote(part.at[0], part_in.at[0], part_ss.at[0], part_rs.at[0], sub=s_down),
        remote(part.at[1], part_in.at[1], part_ss.at[1], part_rs.at[1], sub=s_up),
    ]
    for copy in part_copies:
        copy.start()
    csrc[0:c_edges, :] = column_of(cs[...])
    cs_copy.wait()
    csrc[c_edges:, :] = column_of(cs_other[...])
    tgt_pick = ones_where(
        column_of(ct[...])[:, 0:coarse]
        == lax.broadcasted_iota(jnp.int32, (c_edges, coarse), 1)
    )
    tgt_sum = sum_matrix(ct[...], coarse)
    for i in (6, 7, 8, 9):
        loads[i].wait()
    for copy in part_copies:
        copy.wait()
    own[...] = (
        0.25
        * (
            partial[coarse : 2 * coarse]
            + part_in[0].astype(F32)
            + part_in[1].astype(F32)
        )
    ).astype(BF)

    def gather_parts(g, col):
        ss = lambda i: ag_ss.at[g, i]
        rs = lambda i: ag_rs.at[g, i]

        def send(src, dst, i, target):
            return remote(src, dst, ss(i), rs(i), sub=target)

        def arrived(i, ref):
            remote(ref, ref, ss(i), rs(i), sub=sibling).wait_recv()

        def lines(k, q):
            return col.at[k, GROUPS[q][0] : GROUPS[q][1]]

        def z_send(k, i, step):
            offset = ORDER[i] - step
            to = ORDER.index(offset if offset < 4 else -4)
            return send(col.at[k, i], col.at[k, to], (32 if k else 0) + to, dev_z[step])

        def z_near(k):
            return [z_send(k, 0, step) for step in (1, -1, 2, -2)]

        def z_beyond(k, i):
            if i == 3:
                steps = (1,) if k else (1, 2)
            else:
                steps = (-1, -2) if k else (-1,)
            return [z_send(k, i, step) for step in steps]

        def x_sends(q):
            return [
                send(lines(0, q), lines(3, q), 8 + q, dev_x[1]),
                send(lines(0, q), lines(1, q), 12 + q, dev_x[3]),
            ]

        def x_far():
            return [send(col.at[0, 0], col.at[2, 0], 24, dev_x[2])]

        def choice_send():
            return [send(choice.at[g], choice_in.at[g], 20, sibling)]

        def start(copies):
            for copy in copies:
                copy.start()

        def z_arrived(k, i):
            arrived((32 if k else 0) + i, col.at[k, i])

        def begin():
            start(x_far() + z_near(0) + x_sends(0))

        def forward():
            for i in (3, 4):
                z_arrived(0, i)
                start(z_beyond(0, i))
            arrived(24, col.at[2, 0])
            start(z_near(2))
            for i in (1, 2):
                z_arrived(0, i)
            start(x_sends(1))
            for i in (3, 4):
                z_arrived(2, i)
                start(z_beyond(2, i))
            for i in (5, 6, 7):
                z_arrived(0, i)
            start(x_sends(2))

        def beside():
            for q in range(3):
                arrived(8 + q, lines(3, q))
                arrived(12 + q, lines(1, q))

        def far():
            for i in (1, 2, 5, 6, 7):
                z_arrived(2, i)

        def exchange(theirs):
            choice[g] = theirs
            start(choice_send())

        def exchanged():
            arrived(20, choice_in.at[g])
            return choice_in[g]

        def finish():
            copies = x_far() + choice_send()
            for q in range(3):
                copies += x_sends(q)
            for k in (0, 2):
                copies += z_near(k) + z_beyond(k, 3) + z_beyond(k, 4)
            for copy in copies:
                copy.wait_send()

        return begin, forward, beside, far, exchange, exchanged, finish

    lane = lax.broadcasted_iota(jnp.int32, (1, NZ * coarse), 1)
    turn = lane // coarse
    ahead = jnp.where(lax.rem(turn, 2) == 1, -((turn + 1) // 2), turn // 2)
    span = 2 * coarse
    line_ids = lax.rem(z + ahead + NZ, NZ) * span + c * coarse + lax.rem(lane, coarse)

    finishes = []
    for g, col in enumerate((col0, col1)):
        begin, forward, beside, far, exchange, exchanged, finish = gather_parts(g, col)
        mine = own[...]
        col[0, 0] = mine
        begin()
        picked_own = dot(tgt_pick, mine).astype(BF)
        c_pre = dot(cev[...], wef[1, 0:w]) + dot(picked_own, wef[1, 2 * w : 3 * w])
        n_pre = dot(mine, wnf[1, 0:w])

        def chosen_rows(k, rows):
            labels = jnp.concatenate([csrc[rows, :]] * (NZ * coarse // 128), axis=1)
            return dot(
                ones_where(labels == line_ids + xs[k] * (NZ * span)),
                col[k].reshape(NZ * coarse, w),
            )

        everyone = slice(0, 2 * c_edges)
        forward()
        fetched = chosen_rows(0, everyone)
        beside()
        fetched += chosen_rows(3, everyone) + chosen_rows(1, everyone)
        far()
        exchange((fetched[c_edges:] + chosen_rows(2, slice(c_edges, 2 * c_edges))).astype(BF))
        fetched = fetched[0:c_edges] + chosen_rows(2, slice(0, c_edges))
        fetched += exchanged().astype(F32)
        v = c_pre + dot(fetched.astype(BF), wef[1, w : 2 * w])
        message = layer_norm(dot(silu(v).astype(BF), we2[1]), edge_gain[1:2])
        new_edges = (cev[...].astype(F32) + message).astype(BF)
        cev[...] = new_edges
        summed = dot(tgt_sum, new_edges).astype(BF)
        v = n_pre + dot(summed, wnf[1, w : 2 * w])
        update = layer_norm(dot(silu(v).astype(BF), wn2[1]), node_gain[1:2])
        own[...] = (mine.astype(F32) + update).astype(BF)
        finishes.append(finish)

    sb[1] = own[...]
    sb[3] = jnp.zeros_like(sb[3])
    set_copies = [
        remote(sb.at[1], sb.at[0], set_ss.at[0], set_rs.at[0], sub=s_up),
        remote(sb.at[1], sb.at[2], set_ss.at[1], set_rs.at[1], sub=s_down),
    ]
    for copy in set_copies:
        copy.start()
    chosen = pick_matrix(column_of(slots), 4 * coarse)
    for finish in finishes:
        finish()
    for copy in set_copies:
        copy.wait()
    lifted = dot(sb[...].reshape(4 * coarse, w), wlw[...])
    high = lifted.astype(BF)
    low = (lifted - high.astype(F32)).astype(BF)
    outv[...] = (refined[...].astype(F32) + dot(chosen, high) + dot(chosen, low)).astype(BF)
    copy = pltpu.make_async_copy(outv, out.at[0], out_sem)
    copy.start()
    copy.wait()


def per_device(*arrays):
    fn, fe = arrays[0], arrays[1]
    nodes, w = fn.shape[1], fn.shape[2]
    edges = fe.shape[1]
    halo_rows = arrays[5].shape[2]
    c_edges = arrays[7].shape[1]
    coarse = nodes // 16
    any_space = pl.BlockSpec(memory_space=pl.ANY)
    vmem = pl.BlockSpec(memory_space=pltpu.VMEM)
    big = {0, 1, 7, 10, 11, 13, 14, 16}
    specs = [any_space if i in big else vmem for i in range(17)]
    V = pltpu.VMEM
    D = pltpu.SemaphoreType.DMA
    scratch = [
        V((nodes, w), BF),
        V((edges, w), BF),
        V((2, 3 * w, w), BF),
        V((2, w, w), BF),
        V((2, 2 * w, w), BF),
        V((2, w, w), BF),
        V((w, w), BF),
        V((c_edges, w), BF),
        V((nodes, w), BF),
        V((nodes, w), BF),
        V((4, halo_rows, w), BF),
        V((4, halo_rows, w), BF),
        V((edges, w), F32),
        V((edges, 128), jnp.int32),
        V((edges, 128), jnp.int32),
        V((nodes, w), F32),
        V((nodes, w), F32),
        V((nodes, w), BF),
        V((2, coarse, w), BF),
        V((2, coarse, w), BF),
        V((NX, NZ, coarse, w), BF),
        V((NX, NZ, coarse, w), BF),
        V((2, c_edges, w), BF),
        V((2, c_edges, w), BF),
        V((coarse, w), BF),
        V((2 * c_edges, 128), jnp.int32),
        V((1, c_edges), jnp.int32),
        V((4, coarse, w), BF),
        V((nodes, w), BF),
        D((10,)),
        D,
        D((4,)),
        D((4,)),
        D((2,)),
        D((2,)),
        D((2, 40)),
        D((2, 40)),
        D((2,)),
        D((2,)),
    ]
    return pl.pallas_call(
        kernel,
        out_shape=jax.ShapeDtypeStruct((1, nodes, w), BF),
        in_specs=specs,
        out_specs=any_space,
        scratch_shapes=scratch,
        compiler_params=pltpu.CompilerParams(
            collective_id=0, has_side_effects=True, vmem_limit_bytes=56 * 1024 * 1024
        ),
        cost_estimate=pl.CostEstimate(
            flops=9_000_000_000, bytes_accessed=12_000_000, transcendentals=2_000_000
        ),
    )(*arrays)


def solution(mesh):
    row = P("dom", "sub")
    wide = P("dom", "sub", None)
    placed = (
        wide, wide, row, row, row, wide, row, wide, row, row,
        P(), P(), P(), P(), P(), P(), P(),
    )
    return jax.shard_map(
        per_device, mesh=mesh, in_specs=placed, out_specs=wide, check_vma=False
    )
```

time: 308 us -> 69.9 us (0.23); the launches traced: 303 us -> 68.6 us
  waiting for transfers between devices: 204 us -> 0 us
  Pallas kernels: 0 us -> 66.1 us
  matrix products: 32.2 us -> 0 us
  local copies, waits for them, and re-layouts: 28.3 us -> 1.87 us
  starting transfers between devices: 18 us -> 0 us
  between operations: 14 us -> 0.66 us
  other arithmetic: 5.2 us -> 0 us
    all_gather x2 -> x0, waiting for transfers between devices: 198 us -> none  [collect(): return lax.all_gather(coarse_own, 'sub', axis=0, tiled=True)]
    pallas_call x0 -> x1, Pallas kernels: none -> 66.1 us  [per_device(): pl.pallas_call(kernel, out_shape=jax.ShapeDtypeStruct((1, nodes, w), BF),...]
    dot_general x20 -> x0, matrix products: 32.2 us -> none  [the longest x6 10.1 us: two_layer(): jnp.dot(hidden, weight_out, preferred_element_type=jnp.float32)]
    gather x8 -> x0, local copies, waits for them, and re-layouts: 19.6 us -> none  [the longest x2 6.14 us: per_device(): column[coarse_from]]
    ppermute x8 -> x0, starting transfers between devices: 17.8 us -> none  [the longest x4 11.3 us: extended(): lax.ppermute(tail, axis, [(i, (i + 1) % count) for i in range(ends)])]
    ppermute x8 -> x0, waiting for transfers between devices: 5.38 us -> none  [the longest x4 5.37 us: extended(): lax.ppermute(head, axis, [((i + 1) % count, i) for i in range(ends)])]
    unnamed x44 -> x1, local copies, waits for them, and re-layouts: 5.96 us -> 1.87 us
  transfers between devices with their start and end apart: 10 -> 0, of which waited for: 4 -> 0; matrix products, arithmetic and copies ran while one was open for 6% -> 0% of each run, Pallas kernels for 0% -> 0%
where the time goes in v1:
time: 69.9 us; the launch traced here: 68.6 us
  Pallas kernels  66.1 us (95%)
  local copies, waits for them, and re-layouts  1.87 us (3%)
    pallas_call x1, Pallas kernels, per_device(): pl.pallas_call(kernel, out_shape=jax.ShapeDtypeStruct((1, nodes, w), BF),...  66.1 us
    unnamed x1, local copies, waits for them, and re-layouts  1.87 us

profile of v1, /device:TPU:16, one launch (start us, length us, event | category | flops | bytes accessed | tf_op | source)
XLA Modules:
  0.0 68.6 jit_solution(16861392379684248679)
XLA Ops:
  0.7 66.1 %shard_map.163 = bf16[1,512,512]{2,1,0:T(8,128)(2,1)} custom-call(bf16[1,512,512]{2,1,0:T(8,128)(2,1)} %fn.1, bf16[1,2048,512]{2,1,0:T(8,128)(2,1)} %fe.1, s32[1,2048]{1,0:T(1,128)} %es.1, s32[1,2048]{1,0:T(1,128)} %et.1, s32[1,1]{1,0:T(1,128)S(6)} %copy.19.eb, s32[1,4,128]{2,1,0:T(4,128)} %sr.1, s32[1,512]{1,0:T(1,128)} %cm.1, bf16[1,256,512]{2,1,0:T(8,128)(2,1)} %ce.1, ...), custom_call_target="tpu_custom_call" | custom-call | flops 8999999488 | bytes 12000000 | tf_op jit(solution)/shard_map/pallas_call | solution.py:425
  66.7 1.9 %copy.20 = bf16[1,512,512]{2,1,0:T(8,128)(2,1)} copy(bf16[1,512,512]{2,1,0:T(8,128)(2,1)} %shard_map.163) | data formatting | bytes 1048576

commit v2 on v1

--- a/solution.py
+++ b/solution.py
@@ -54,12 +54,13 @@
 
 
 def kernel(
-    fn, fe, es, et, eb, sr, cm, ce, cs, ct, ef, e2, eg, nf, n2, ng, lw,
+    fn, fe, es_far, et_far, eb, sr_far, cm_far, ce, cs_far, ct_far, ef, e2, eg_far, nf, n2, ng_far, lw,
     out,
+    es, et, sr, cm, cs, ct, eg, ng,
     states, lat, wef, we2, wnf, wn2, wlw, cev,
     a_own, b_tgt, pick, halo, pre, src_col, tgt_col, agg, node_pre, refined,
     part, part_in, col0, col1, choice, choice_in, own, csrc, cs_other, sb, outv,
-    load_sem, out_sem, halo_ss, halo_rs, part_ss, part_rs, ag_ss, ag_rs, set_ss, set_rs,
+    load_sem, label_sem, out_sem, halo_ss, halo_rs, part_ss, part_rs, ag_ss, ag_rs, set_ss, set_rs,
 ):
     s = lax.axis_index("sub")
     d = lax.axis_index("dom")
@@ -84,6 +85,15 @@
     for partner in (d_up, d_down):
         pl.semaphore_signal(barrier, inc=1, device_id={"dom": partner}, device_id_type=MESH)
 
+    labels = [
+        pltpu.make_async_copy(a, b, label_sem.at[i])
+        for i, (a, b) in enumerate(
+            [
+                (sr_far, sr), (es_far, es), (et_far, et), (cs_far, cs),
+                (cm_far, cm), (ct_far, ct), (eg_far, eg), (ng_far, ng),
+            ]
+        )
+    ]
     pairs = [
         (fn.at[0], states),
         (ef.at[0], wef.at[0]),
@@ -97,7 +107,7 @@
         (lw, wlw),
     ]
     loads = [pltpu.make_async_copy(a, b, load_sem.at[i]) for i, (a, b) in enumerate(pairs)]
-    for copy in loads:
+    for copy in loads[:2] + labels + loads[2:]:
         copy.start()
 
     w = states.shape[1]
@@ -116,6 +126,8 @@
     loads[0].wait()
     loads[1].wait()
     a_own[...] = dot(states[...], wef[0, w : 2 * w]).astype(BF)
+    for copy in labels:
+        copy.wait()
     listed = jnp.concatenate([column_of(sr[0, k : k + 1, :]) for k in range(4)], axis=0)
     picked = dot(pick_matrix(listed, nodes), a_own[...]).astype(BF)
     pick[...] = picked.reshape(4, halo_rows, w)
@@ -147,7 +159,7 @@
         )
         return carry
 
-    lax.fori_loop(0, blocks, first, 0)
+    lax.fori_loop(0, blocks, first, 0, unroll=True)
     loads[4].wait()
     node_pre[...] = dot(states[...], wnf[0, 0:w])
     loads[3].wait()
@@ -173,7 +185,7 @@
         agg[...] += dot(sum_matrix(targets, nodes), renewed)
         return carry
 
-    lax.fori_loop(0, blocks, second, 0)
+    lax.fori_loop(0, blocks, second, 0, unroll=True)
 
     loads[5].wait()
     v = node_pre[...] + dot(agg[...].astype(BF), wnf[0, w : 2 * w])
@@ -229,13 +241,13 @@
             return send(col.at[k, i], col.at[k, to], (32 if k else 0) + to, dev_z[step])
 
         def z_near(k):
-            return [z_send(k, 0, step) for step in (1, -1, 2, -2)]
+            return [z_send(k, 0, step) for step in (2, -2, 1, -1)]
 
         def z_beyond(k, i):
             if i == 3:
-                steps = (1,) if k else (1, 2)
+                steps = (1,) if k else (2, 1)
             else:
-                steps = (-1, -2) if k else (-1,)
+                steps = (-2, -1) if k else (-1,)
             return [z_send(k, i, step) for step in steps]
 
         def x_sends(q):
@@ -362,10 +374,16 @@
     lifted = dot(sb[...].reshape(4 * coarse, w), wlw[...])
     high = lifted.astype(BF)
     low = (lifted - high.astype(F32)).astype(BF)
-    outv[...] = (refined[...].astype(F32) + dot(chosen, high) + dot(chosen, low)).astype(BF)
-    copy = pltpu.make_async_copy(outv, out.at[0], out_sem)
-    copy.start()
-    copy.wait()
+    halves = []
+    for i in range(2):
+        rows = slice(i * (nodes // 2), (i + 1) * (nodes // 2))
+        outv[rows, :] = (
+            refined[rows, :].astype(F32) + dot(chosen[rows], high) + dot(chosen[rows], low)
+        ).astype(BF)
+        halves.append(pltpu.make_async_copy(outv.at[rows], out.at[0, rows], out_sem.at[i]))
+        halves[i].start()
+    for copy in halves:
+        copy.wait()
 
 
 def per_device(*arrays):
@@ -375,13 +393,20 @@
     halo_rows = arrays[5].shape[2]
     c_edges = arrays[7].shape[1]
     coarse = nodes // 16
-    any_space = pl.BlockSpec(memory_space=pl.ANY)
-    vmem = pl.BlockSpec(memory_space=pltpu.VMEM)
-    big = {0, 1, 7, 10, 11, 13, 14, 16}
-    specs = [any_space if i in big else vmem for i in range(17)]
+    far = pl.BlockSpec(memory_space=pl.ANY)
+    near = pl.BlockSpec(memory_space=pltpu.VMEM)
+    specs = [near if i == 4 else far for i in range(17)]
     V = pltpu.VMEM
     D = pltpu.SemaphoreType.DMA
     scratch = [
+        V((1, edges), jnp.int32),
+        V((1, edges), jnp.int32),
+        V((1, 4, halo_rows), jnp.int32),
+        V((1, nodes), jnp.int32),
+        V((1, c_edges), jnp.int32),
+        V((1, c_edges), jnp.int32),
+        V((2, w), BF),
+        V((2, w), BF),
         V((nodes, w), BF),
         V((edges, w), BF),
         V((2, 3 * w, w), BF),
@@ -412,7 +437,8 @@
         V((4, coarse, w), BF),
         V((nodes, w), BF),
         D((10,)),
-        D,
+        D((8,)),
+        D((2,)),
         D((4,)),
         D((4,)),
         D((2,)),
@@ -426,7 +452,7 @@
         kernel,
         out_shape=jax.ShapeDtypeStruct((1, nodes, w), BF),
         in_specs=specs,
-        out_specs=any_space,
+        out_specs=far,
         scratch_shapes=scratch,
         compiler_params=pltpu.CompilerParams(
             collective_id=0, has_side_effects=True, vmem_limit_bytes=56 * 1024 * 1024

time: 69.9 us -> 68.9 us (0.986)
  the two profiles are of different devices: /device:TPU:16 before, /device:TPU:0 now
where the time goes in v2:
time: 68.9 us; the launch traced here: 68.7 us
  Pallas kernels  66.2 us (96%)
  local copies, waits for them, and re-layouts  1.87 us (3%)
    pallas_call x1, Pallas kernels, per_device(): pl.pallas_call(kernel, out_shape=jax.ShapeDtypeStruct((1, nodes, w), BF),...  66.2 us
    unnamed x1, local copies, waits for them, and re-layouts  1.87 us

profile of v2, /device:TPU:0, one launch (start us, length us, event | category | flops | bytes accessed | tf_op | source)
XLA Modules:
  0.0 68.7 jit_solution(2866996634092630029)
XLA Ops:
  0.7 66.2 %shard_map.163 = bf16[1,512,512]{2,1,0:T(8,128)(2,1)} custom-call(bf16[1,512,512]{2,1,0:T(8,128)(2,1)} %fn.1, bf16[1,2048,512]{2,1,0:T(8,128)(2,1)} %fe.1, s32[1,2048]{1,0:T(1,128)} %es_far.1, s32[1,2048]{1,0:T(1,128)} %et_far.1, s32[1,1]{1,0:T(1,128)S(6)} %copy.19.eb, s32[1,4,128]{2,1,0:T(4,128)} %sr_far.1, s32[1,512]{1,0:T(1,128)} %cm_far.1, ...), custom_call_target="tpu_custom_call" | custom-call | flops 8999999488 | bytes 12000000 | tf_op jit(solution)/shard_map/pallas_call | solution.py:451
  66.9 1.9 %copy.20 = bf16[1,512,512]{2,1,0:T(8,128)(2,1)} copy(bf16[1,512,512]{2,1,0:T(8,128)(2,1)} %shard_map.163) | data formatting | bytes 1048576

commit v3 on v2

--- a/solution.py
+++ b/solution.py
@@ -21,11 +21,16 @@
 
 
 def silu(v):
-    return 0.5 * v * (1.0 + jnp.tanh(0.5 * v))
-
-
-def layer_norm(v, gain):
-    centre = v - jnp.mean(v, axis=-1, keepdims=True)
+    half = 0.5 * v
+    return half + half * jnp.tanh(half)
+
+
+def centred(weight):
+    wide = weight.astype(F32)
+    return (wide - jnp.mean(wide, axis=-1, keepdims=True)).astype(BF)
+
+
+def scaled(centre, gain):
     variance = jnp.mean(centre * centre, axis=-1, keepdims=True)
     return centre * lax.rsqrt(variance + EPSILON) * gain
 
@@ -35,22 +40,24 @@
     parts = [
         jnp.transpose(jnp.broadcast_to(row[:, i : i + 128], (128, 128))) for i in range(0, n, 128)
     ]
-    return parts[0] if len(parts) == 1 else jnp.concatenate(parts, axis=0)
+    return (parts[0] if len(parts) == 1 else jnp.concatenate(parts, axis=0)).astype(jnp.int16)
 
 
 def ones_where(mask):
-    return jnp.where(mask, 1.0, 0.0).astype(BF)
+    return jnp.where(mask, jnp.ones((), BF), jnp.zeros((), BF))
 
 
 def pick_matrix(col, lanes, offset=0):
     reps = lanes // 128
     wide = col if reps == 1 else jnp.concatenate([col] * reps, axis=1)
-    return ones_where(wide == lax.broadcasted_iota(jnp.int32, wide.shape, 1) + offset)
+    ids = (lax.broadcasted_iota(jnp.int32, wide.shape, 1) + offset).astype(jnp.int16)
+    return ones_where(wide == ids)
 
 
 def sum_matrix(row, rows):
     shape = (rows, row.shape[1])
-    return ones_where(jnp.broadcast_to(row, shape) == lax.broadcasted_iota(jnp.int32, shape, 0))
+    rows_of = lax.broadcasted_iota(jnp.int32, shape, 0).astype(jnp.int16)
+    return ones_where(jnp.broadcast_to(row.astype(jnp.int16), shape) == rows_of)
 
 
 def kernel(
@@ -58,7 +65,7 @@
     out,
     es, et, sr, cm, cs, ct, eg, ng,
     states, lat, wef, we2, wnf, wn2, wlw, cev,
-    a_own, b_tgt, pick, halo, pre, src_col, tgt_col, agg, node_pre, refined,
+    a_own, b_tgt, pick, halo, pre, src_col, tgt_col, node_pre, refined,
     part, part_in, col0, col1, choice, choice_in, own, csrc, cs_other, sb, outv,
     load_sem, label_sem, out_sem, halo_ss, halo_rs, part_ss, part_rs, ag_ss, ag_rs, set_ss, set_rs,
 ):
@@ -163,13 +170,15 @@
     loads[4].wait()
     node_pre[...] = dot(states[...], wnf[0, 0:w])
     loads[3].wait()
+    we2[0] = centred(we2[0])
+    loads[5].wait()
+    wn2[0] = centred(wn2[0])
 
     for copy in halo_copies:
         copy.wait()
     exists = (s > 0, s < subs - 1, d > 0, d < 3)
     for k in range(4):
         halo[k] = jnp.where(exists[k], halo[k].astype(F32), 0.0).astype(BF)
-    agg[...] = jnp.zeros_like(agg)
     edge_gain = eg[...].astype(F32)
     node_gain = ng[...].astype(F32)
     used = eb[...]
@@ -179,17 +188,17 @@
         here = pl.ds(start, nodes)
         table = halo[...].reshape(4 * halo_rows, w)
         v = pre[here, :] + dot(pick_matrix(src_col[here, :], 4 * halo_rows, nodes), table)
-        message = layer_norm(dot(silu(v).astype(BF), we2[0]), edge_gain[0:1])
-        renewed = (lat[here, :].astype(F32) + message).astype(BF)
-        targets = jnp.where(b < used, et[:, here], -1)
-        agg[...] += dot(sum_matrix(targets, nodes), renewed)
+        message = scaled(dot(silu(v).astype(BF), we2[0]), edge_gain[0:1])
+        lat[here, :] = (lat[here, :].astype(F32) + message).astype(BF)
         return carry
 
     lax.fori_loop(0, blocks, second, 0, unroll=True)
 
-    loads[5].wait()
-    v = node_pre[...] + dot(agg[...].astype(BF), wnf[0, w : 2 * w])
-    update = layer_norm(dot(silu(v).astype(BF), wn2[0]), node_gain[0:1])
+    block = lax.broadcasted_iota(jnp.int32, (1, edges), 1) // nodes
+    targets = jnp.where(block < used, et[...], -1)
+    summed = dot(sum_matrix(targets, nodes), lat[...]).astype(BF)
+    v = node_pre[...] + dot(summed, wnf[0, w : 2 * w])
+    update = scaled(dot(silu(v).astype(BF), wn2[0]), node_gain[0:1])
     refined[...] = (states[...].astype(F32) + update).astype(BF)
     slots = cm[...] - (s - 1) * coarse
     partial = dot(sum_matrix(slots, 3 * coarse), refined[...])
@@ -206,11 +215,13 @@
     csrc[c_edges:, :] = column_of(cs_other[...])
     tgt_pick = ones_where(
         column_of(ct[...])[:, 0:coarse]
-        == lax.broadcasted_iota(jnp.int32, (c_edges, coarse), 1)
+        == lax.broadcasted_iota(jnp.int32, (c_edges, coarse), 1).astype(jnp.int16)
     )
     tgt_sum = sum_matrix(ct[...], coarse)
     for i in (6, 7, 8, 9):
         loads[i].wait()
+    we2[1] = centred(we2[1])
+    wn2[1] = centred(wn2[1])
     for copy in part_copies:
         copy.wait()
     own[...] = (
@@ -335,7 +346,7 @@
         def chosen_rows(k, rows):
             labels = jnp.concatenate([csrc[rows, :]] * (NZ * coarse // 128), axis=1)
             return dot(
-                ones_where(labels == line_ids + xs[k] * (NZ * span)),
+                ones_where(labels == (line_ids + xs[k] * (NZ * span)).astype(jnp.int16)),
                 col[k].reshape(NZ * coarse, w),
             )
 
@@ -349,12 +360,12 @@
         fetched = fetched[0:c_edges] + chosen_rows(2, slice(0, c_edges))
         fetched += exchanged().astype(F32)
         v = c_pre + dot(fetched.astype(BF), wef[1, w : 2 * w])
-        message = layer_norm(dot(silu(v).astype(BF), we2[1]), edge_gain[1:2])
+        message = scaled(dot(silu(v).astype(BF), we2[1]), edge_gain[1:2])
         new_edges = (cev[...].astype(F32) + message).astype(BF)
         cev[...] = new_edges
         summed = dot(tgt_sum, new_edges).astype(BF)
         v = n_pre + dot(summed, wnf[1, w : 2 * w])
-        update = layer_norm(dot(silu(v).astype(BF), wn2[1]), node_gain[1:2])
+        update = scaled(dot(silu(v).astype(BF), wn2[1]), node_gain[1:2])
         own[...] = (mine.astype(F32) + update).astype(BF)
         finishes.append(finish)
 
@@ -420,9 +431,8 @@
         V((4, halo_rows, w), BF),
         V((4, halo_rows, w), BF),
         V((edges, w), F32),
-        V((edges, 128), jnp.int32),
-        V((edges, 128), jnp.int32),
-        V((nodes, w), F32),
+        V((edges, 128), jnp.int16),
+        V((edges, 128), jnp.int16),
         V((nodes, w), F32),
         V((nodes, w), BF),
         V((2, coarse, w), BF),
@@ -432,7 +442,7 @@
         V((2, c_edges, w), BF),
         V((2, c_edges, w), BF),
         V((coarse, w), BF),
-        V((2 * c_edges, 128), jnp.int32),
+        V((2 * c_edges, 128), jnp.int16),
         V((1, c_edges), jnp.int32),
         V((4, coarse, w), BF),
         V((nodes, w), BF),

time: 68.9 us -> 67.2 us (0.975)
  Pallas kernels: 66.2 us -> 64.6 us
    pallas_call x1, Pallas kernels: 66.2 us -> 64.6 us  [per_device(): pl.pallas_call(kernel, out_shape=jax.ShapeDtypeStruct((1, nodes, w), BF),...]
where the time goes in v3:
time: 67.2 us; the launch traced here: 67.1 us
  Pallas kernels  64.6 us (96%)
  local copies, waits for them, and re-layouts  1.87 us (3%)
    pallas_call x1, Pallas kernels, per_device(): pl.pallas_call(kernel, out_shape=jax.ShapeDtypeStruct((1, nodes, w), BF),...  64.6 us
    unnamed x1, local copies, waits for them, and re-layouts  1.87 us

profile of v3, /device:TPU:0, one launch (start us, length us, event | category | flops | bytes accessed | tf_op | source)
XLA Modules:
  0.0 67.1 jit_solution(10578251645901971472)
XLA Ops:
  0.7 64.6 %shard_map.163 = bf16[1,512,512]{2,1,0:T(8,128)(2,1)} custom-call(bf16[1,512,512]{2,1,0:T(8,128)(2,1)} %fn.1, bf16[1,2048,512]{2,1,0:T(8,128)(2,1)} %fe.1, s32[1,2048]{1,0:T(1,128)} %es_far.1, s32[1,2048]{1,0:T(1,128)} %et_far.1, s32[1,1]{1,0:T(1,128)S(6)} %copy.19.eb, s32[1,4,128]{2,1,0:T(4,128)} %sr_far.1, s32[1,512]{1,0:T(1,128)} %cm_far.1, ...), custom_call_target="tpu_custom_call" | custom-call | flops 8999999488 | bytes 12000000 | tf_op jit(solution)/shard_map/pallas_call | solution.py:461
  65.2 1.9 %copy.20 = bf16[1,512,512]{2,1,0:T(8,128)(2,1)} copy(bf16[1,512,512]{2,1,0:T(8,128)(2,1)} %shard_map.163) | data formatting | bytes 1048576

commit v4 on v3

--- a/solution.py
+++ b/solution.py
@@ -101,12 +101,15 @@
             ]
         )
     ]
+    w = states.shape[1]
     pairs = [
         (fn.at[0], states),
-        (ef.at[0], wef.at[0]),
+        (ef.at[0, w : 2 * w], wef.at[0, w : 2 * w]),
+        (ef.at[0, 2 * w : 3 * w], wef.at[0, 2 * w : 3 * w]),
+        (ef.at[0, 0:w], wef.at[0, 0:w]),
         (fe.at[0], lat),
+        (nf.at[0], wnf.at[0]),
         (e2, we2),
-        (nf.at[0], wnf.at[0]),
         (n2, wn2),
         (ce.at[0], cev),
         (ef.at[1], wef.at[1]),
@@ -114,10 +117,9 @@
         (lw, wlw),
     ]
     loads = [pltpu.make_async_copy(a, b, load_sem.at[i]) for i, (a, b) in enumerate(pairs)]
-    for copy in loads[:2] + labels + loads[2:]:
+    for copy in labels[:3] + loads[:2] + labels[3:] + loads[2:]:
         copy.start()
 
-    w = states.shape[1]
     nodes = states.shape[0]
     halo_rows = halo.shape[1]
     coarse = own.shape[0]
@@ -130,14 +132,19 @@
             device_id=device, device_id_type=MESH,
         )
 
+    for copy in labels[:3]:
+        copy.wait()
+    listed = jnp.concatenate([column_of(sr[0, k : k + 1, :]) for k in range(4)], axis=0)
+    wanted = pick_matrix(listed, nodes)
+    tgt_col[...] = column_of(et[...])
+    src_col[...] = column_of(es[...])
     loads[0].wait()
     loads[1].wait()
     a_own[...] = dot(states[...], wef[0, w : 2 * w]).astype(BF)
-    for copy in labels:
-        copy.wait()
-    listed = jnp.concatenate([column_of(sr[0, k : k + 1, :]) for k in range(4)], axis=0)
-    picked = dot(pick_matrix(listed, nodes), a_own[...]).astype(BF)
+    picked = dot(wanted, a_own[...]).astype(BF)
     pick[...] = picked.reshape(4, halo_rows, w)
+    for copy in labels[3:]:
+        copy.wait()
     pl.semaphore_wait(barrier, 11)
     halo_copies = [
         remote(pick.at[1], halo.at[0], halo_ss.at[0], halo_rs.at[0], sub=s_up),
@@ -150,11 +157,11 @@
     cs_copy = remote(cs, cs_other, ag_ss.at[0, 21], ag_rs.at[0, 21], sub=sibling)
     cs_copy.start()
 
+    loads[2].wait()
     b_tgt[...] = dot(states[...], wef[0, 2 * w : 3 * w]).astype(BF)
     edges = lat.shape[0]
-    src_col[...] = column_of(es[...])
-    tgt_col[...] = column_of(et[...])
-    loads[2].wait()
+    loads[3].wait()
+    loads[4].wait()
     blocks = edges // nodes
 
     def first(b, carry):
@@ -167,11 +174,11 @@
         return carry
 
     lax.fori_loop(0, blocks, first, 0, unroll=True)
-    loads[4].wait()
+    loads[5].wait()
     node_pre[...] = dot(states[...], wnf[0, 0:w])
-    loads[3].wait()
+    loads[6].wait()
     we2[0] = centred(we2[0])
-    loads[5].wait()
+    loads[7].wait()
     wn2[0] = centred(wn2[0])
 
     for copy in halo_copies:
@@ -218,7 +225,7 @@
         == lax.broadcasted_iota(jnp.int32, (c_edges, coarse), 1).astype(jnp.int16)
     )
     tgt_sum = sum_matrix(ct[...], coarse)
-    for i in (6, 7, 8, 9):
+    for i in (8, 9, 10, 11):
         loads[i].wait()
     we2[1] = centred(we2[1])
     wn2[1] = centred(wn2[1])
@@ -292,12 +299,12 @@
             for i in (1, 2):
                 z_arrived(0, i)
             start(x_sends(1))
+            for i in (5, 6, 7):
+                z_arrived(0, i)
+            start(x_sends(2))
             for i in (3, 4):
                 z_arrived(2, i)
                 start(z_beyond(2, i))
-            for i in (5, 6, 7):
-                z_arrived(0, i)
-            start(x_sends(2))
 
         def beside():
             for q in range(3):
@@ -446,7 +453,7 @@
         V((1, c_edges), jnp.int32),
         V((4, coarse, w), BF),
         V((nodes, w), BF),
-        D((10,)),
+        D((12,)),
         D((8,)),
         D((2,)),
         D((4,)),

time: 67.2 us -> 64.7 us (0.963)
  the two profiles are of different devices: /device:TPU:0 before, /device:TPU:16 now
where the time goes in v4:
time: 64.7 us; the launch traced here: 64.6 us
  Pallas kernels  62.1 us (96%)
  local copies, waits for them, and re-layouts  1.87 us (3%)
  between operations  0.66 us (1%)
    pallas_call x1, Pallas kernels, per_device(): pl.pallas_call(kernel, out_shape=jax.ShapeDtypeStruct((1, nodes, w), BF),...  62.1 us
    unnamed x1, local copies, waits for them, and re-layouts  1.87 us

profile of v4, /device:TPU:16, one launch (start us, length us, event | category | flops | bytes accessed | tf_op | source)
XLA Modules:
  0.0 64.6 jit_solution(10166364973346073220)
XLA Ops:
  0.7 62.1 %shard_map.163 = bf16[1,512,512]{2,1,0:T(8,128)(2,1)} custom-call(bf16[1,512,512]{2,1,0:T(8,128)(2,1)} %fn.1, bf16[1,2048,512]{2,1,0:T(8,128)(2,1)} %fe.1, s32[1,2048]{1,0:T(1,128)} %es_far.1, s32[1,2048]{1,0:T(1,128)} %et_far.1, s32[1,1]{1,0:T(1,128)S(6)} %copy.19.eb, s32[1,4,128]{2,1,0:T(4,128)} %sr_far.1, s32[1,512]{1,0:T(1,128)} %cm_far.1, ...), custom_call_target="tpu_custom_call" | custom-call | flops 8999999488 | bytes 12000000 | tf_op jit(solution)/shard_map/pallas_call | solution.py:468
  62.7 1.9 %copy.20 = bf16[1,512,512]{2,1,0:T(8,128)(2,1)} copy(bf16[1,512,512]{2,1,0:T(8,128)(2,1)} %shard_map.163) | data formatting | bytes 1048576

commit v5 on v4

--- a/solution.py
+++ b/solution.py
@@ -66,7 +66,7 @@
     es, et, sr, cm, cs, ct, eg, ng,
     states, lat, wef, we2, wnf, wn2, wlw, cev,
     a_own, b_tgt, pick, halo, pre, src_col, tgt_col, node_pre, refined,
-    part, part_in, col0, col1, choice, choice_in, own, csrc, cs_other, sb, outv,
+    part, part_in, col0, col1, choice, choice_in, own, csrc, cs_other, wants, sb, outv,
     load_sem, label_sem, out_sem, halo_ss, halo_rs, part_ss, part_rs, ag_ss, ag_rs, set_ss, set_rs,
 ):
     s = lax.axis_index("sub")
@@ -227,8 +227,6 @@
     tgt_sum = sum_matrix(ct[...], coarse)
     for i in (8, 9, 10, 11):
         loads[i].wait()
-    we2[1] = centred(we2[1])
-    wn2[1] = centred(wn2[1])
     for copy in part_copies:
         copy.wait()
     own[...] = (
@@ -338,6 +336,7 @@
     turn = lane // coarse
     ahead = jnp.where(lax.rem(turn, 2) == 1, -((turn + 1) // 2), turn // 2)
     span = 2 * coarse
+    plane = NZ * coarse
     line_ids = lax.rem(z + ahead + NZ, NZ) * span + c * coarse + lax.rem(lane, coarse)
 
     finishes = []
@@ -350,23 +349,22 @@
         c_pre = dot(cev[...], wef[1, 0:w]) + dot(picked_own, wef[1, 2 * w : 3 * w])
         n_pre = dot(mine, wnf[1, 0:w])
 
-        def chosen_rows(k, rows):
-            labels = jnp.concatenate([csrc[rows, :]] * (NZ * coarse // 128), axis=1)
-            return dot(
-                ones_where(labels == (line_ids + xs[k] * (NZ * span)).astype(jnp.int16)),
-                col[k].reshape(NZ * coarse, w),
-            )
-
-        everyone = slice(0, 2 * c_edges)
         forward()
-        fetched = chosen_rows(0, everyone)
+        if g == 0:
+            we2[1] = centred(we2[1])
+            wn2[1] = centred(wn2[1])
+            labels = jnp.concatenate([csrc[...]] * (plane // 128), axis=1)
+            for k in range(NX):
+                ids = (line_ids + xs[k] * (NZ * span)).astype(jnp.int16)
+                wants[:, k * plane : (k + 1) * plane] = ones_where(labels == ids)
+        fetched = dot(wants[:, 0:plane], col[0].reshape(plane, w))
         beside()
-        fetched += chosen_rows(3, everyone) + chosen_rows(1, everyone)
         far()
-        exchange((fetched[c_edges:] + chosen_rows(2, slice(c_edges, 2 * c_edges))).astype(BF))
-        fetched = fetched[0:c_edges] + chosen_rows(2, slice(0, c_edges))
-        fetched += exchanged().astype(F32)
-        v = c_pre + dot(fetched.astype(BF), wef[1, w : 2 * w])
+        others = col[1:NX].reshape((NX - 1) * plane, w)
+        exchange((fetched[c_edges:] + dot(wants[c_edges:, plane:], others)).astype(BF))
+        fetched = (fetched[0:c_edges] + dot(wants[0:c_edges, plane:], others)).astype(BF)
+        c_pre += dot(fetched, wef[1, w : 2 * w])
+        v = c_pre + dot(exchanged(), wef[1, w : 2 * w])
         message = scaled(dot(silu(v).astype(BF), we2[1]), edge_gain[1:2])
         new_edges = (cev[...].astype(F32) + message).astype(BF)
         cev[...] = new_edges
@@ -451,6 +449,7 @@
         V((coarse, w), BF),
         V((2 * c_edges, 128), jnp.int16),
         V((1, c_edges), jnp.int32),
+        V((2 * c_edges, NX * NZ * coarse), BF),
         V((4, coarse, w), BF),
         V((nodes, w), BF),
         D((12,)),

time: 64.7 us -> 65.1 us (level)
  no operation moved by 1% of the time
where the time goes in v5:
time: 65.1 us; the launch traced here: 64.9 us
  Pallas kernels  62.3 us (96%)
  local copies, waits for them, and re-layouts  1.87 us (3%)
  between operations  0.66 us (1%)
    pallas_call x1, Pallas kernels, per_device(): pl.pallas_call(kernel, out_shape=jax.ShapeDtypeStruct((1, nodes, w), BF),...  62.3 us
    unnamed x1, local copies, waits for them, and re-layouts  1.87 us

profile of v5, /device:TPU:16, one launch (start us, length us, event | category | flops | bytes accessed | tf_op | source)
XLA Modules:
  0.0 64.9 jit_solution(16194258782324882799)
XLA Ops:
  0.7 62.3 %shard_map.163 = bf16[1,512,512]{2,1,0:T(8,128)(2,1)} custom-call(bf16[1,512,512]{2,1,0:T(8,128)(2,1)} %fn.1, bf16[1,2048,512]{2,1,0:T(8,128)(2,1)} %fe.1, s32[1,2048]{1,0:T(1,128)} %es_far.1, s32[1,2048]{1,0:T(1,128)} %et_far.1, s32[1,1]{1,0:T(1,128)S(6)} %copy.19.eb, s32[1,4,128]{2,1,0:T(4,128)} %sr_far.1, s32[1,512]{1,0:T(1,128)} %cm_far.1, ...), custom_call_target="tpu_custom_call" | custom-call | flops 8999999488 | bytes 12000000 | tf_op jit(solution)/shard_map/pallas_call | solution.py:467
  63.0 1.9 %copy.20 = bf16[1,512,512]{2,1,0:T(8,128)(2,1)} copy(bf16[1,512,512]{2,1,0:T(8,128)(2,1)} %shard_map.163) | data formatting | bytes 1048576

commit v6 on v5

--- a/solution.py
+++ b/solution.py
@@ -137,7 +137,6 @@
     listed = jnp.concatenate([column_of(sr[0, k : k + 1, :]) for k in range(4)], axis=0)
     wanted = pick_matrix(listed, nodes)
     tgt_col[...] = column_of(et[...])
-    src_col[...] = column_of(es[...])
     loads[0].wait()
     loads[1].wait()
     a_own[...] = dot(states[...], wef[0, w : 2 * w]).astype(BF)
@@ -157,6 +156,7 @@
     cs_copy = remote(cs, cs_other, ag_ss.at[0, 21], ag_rs.at[0, 21], sub=sibling)
     cs_copy.start()
 
+    src_col[...] = column_of(es[...])
     loads[2].wait()
     b_tgt[...] = dot(states[...], wef[0, 2 * w : 3 * w]).astype(BF)
     edges = lat.shape[0]
@@ -256,8 +256,8 @@
             to = ORDER.index(offset if offset < 4 else -4)
             return send(col.at[k, i], col.at[k, to], (32 if k else 0) + to, dev_z[step])
 
-        def z_near(k):
-            return [z_send(k, 0, step) for step in (2, -2, 1, -1)]
+        def z_near(k, steps=(2, -2, 1, -1)):
+            return [z_send(k, 0, step) for step in steps]
 
         def z_beyond(k, i):
             if i == 3:
@@ -289,14 +289,15 @@
             start(x_far() + z_near(0) + x_sends(0))
 
         def forward():
+            arrived(24, col.at[2, 0])
+            start(z_near(2, (2, -2)))
             for i in (3, 4):
                 z_arrived(0, i)
                 start(z_beyond(0, i))
-            arrived(24, col.at[2, 0])
-            start(z_near(2))
             for i in (1, 2):
                 z_arrived(0, i)
             start(x_sends(1))
+            start(z_near(2, (1, -1)))
             for i in (5, 6, 7):
                 z_arrived(0, i)
             start(x_sends(2))

time: 65.1 us -> 66.1 us (1.015)
  Pallas kernels: 62.3 us -> 63.4 us
    pallas_call x1, Pallas kernels: 62.3 us -> 63.4 us  [per_device(): pl.pallas_call(kernel, out_shape=jax.ShapeDtypeStruct((1, nodes, w), BF),...]
where the time goes in v6:
time: 66.1 us; the launch traced here: 66 us
  Pallas kernels  63.4 us (96%)
  local copies, waits for them, and re-layouts  1.87 us (3%)
    pallas_call x1, Pallas kernels, per_device(): pl.pallas_call(kernel, out_shape=jax.ShapeDtypeStruct((1, nodes, w), BF),...  63.4 us
    unnamed x1, local copies, waits for them, and re-layouts  1.87 us

profile of v6, /device:TPU:16, one launch (start us, length us, event | category | flops | bytes accessed | tf_op | source)
XLA Modules:
  0.0 66.0 jit_solution(875222829385027219)
XLA Ops:
  0.7 63.4 %shard_map.163 = bf16[1,512,512]{2,1,0:T(8,128)(2,1)} custom-call(bf16[1,512,512]{2,1,0:T(8,128)(2,1)} %fn.1, bf16[1,2048,512]{2,1,0:T(8,128)(2,1)} %fe.1, s32[1,2048]{1,0:T(1,128)} %es_far.1, s32[1,2048]{1,0:T(1,128)} %et_far.1, s32[1,1]{1,0:T(1,128)S(6)} %copy.19.eb, s32[1,4,128]{2,1,0:T(4,128)} %sr_far.1, s32[1,512]{1,0:T(1,128)} %cm_far.1, ...), custom_call_target="tpu_custom_call" | custom-call | flops 8999999488 | bytes 12000000 | tf_op jit(solution)/shard_map/pallas_call | solution.py:468
  64.1 1.9 %copy.20 = bf16[1,512,512]{2,1,0:T(8,128)(2,1)} copy(bf16[1,512,512]{2,1,0:T(8,128)(2,1)} %shard_map.163) | data formatting | bytes 1048576

commit v7 on v5

--- a/solution.py
+++ b/solution.py
@@ -292,11 +292,11 @@
             for i in (3, 4):
                 z_arrived(0, i)
                 start(z_beyond(0, i))
-            arrived(24, col.at[2, 0])
-            start(z_near(2))
             for i in (1, 2):
                 z_arrived(0, i)
             start(x_sends(1))
+            arrived(24, col.at[2, 0])
+            start(z_near(2))
             for i in (5, 6, 7):
                 z_arrived(0, i)
             start(x_sends(2))

time: 65.1 us -> 65.4 us (level)
  no operation moved by 1% of the time
where the time goes in v7:
time: 65.4 us; the launch traced here: 65.3 us
  Pallas kernels  62.8 us (96%)
  local copies, waits for them, and re-layouts  1.87 us (3%)
  between operations  0.66 us (1%)
    pallas_call x1, Pallas kernels, per_device(): pl.pallas_call(kernel, out_shape=jax.ShapeDtypeStruct((1, nodes, w), BF),...  62.8 us
    unnamed x1, local copies, waits for them, and re-layouts  1.87 us

profile of v7, /device:TPU:16, one launch (start us, length us, event | category | flops | bytes accessed | tf_op | source)
XLA Modules:
  0.0 65.3 jit_solution(11113115623595735532)
XLA Ops:
  0.7 62.8 %shard_map.163 = bf16[1,512,512]{2,1,0:T(8,128)(2,1)} custom-call(bf16[1,512,512]{2,1,0:T(8,128)(2,1)} %fn.1, bf16[1,2048,512]{2,1,0:T(8,128)(2,1)} %fe.1, s32[1,2048]{1,0:T(1,128)} %es_far.1, s32[1,2048]{1,0:T(1,128)} %et_far.1, s32[1,1]{1,0:T(1,128)S(6)} %copy.19.eb, s32[1,4,128]{2,1,0:T(4,128)} %sr_far.1, s32[1,512]{1,0:T(1,128)} %cm_far.1, ...), custom_call_target="tpu_custom_call" | custom-call | flops 8999999488 | bytes 12000000 | tf_op jit(solution)/shard_map/pallas_call | solution.py:467
  63.4 1.9 %copy.20 = bf16[1,512,512]{2,1,0:T(8,128)(2,1)} copy(bf16[1,512,512]{2,1,0:T(8,128)(2,1)} %shard_map.163) | data formatting | bytes 1048576

commit v8 on v4

--- a/solution.py
+++ b/solution.py
@@ -65,7 +65,7 @@
     out,
     es, et, sr, cm, cs, ct, eg, ng,
     states, lat, wef, we2, wnf, wn2, wlw, cev,
-    a_own, b_tgt, pick, halo, pre, src_col, tgt_col, node_pre, refined,
+    pick, halo, pre, src_col, tgt_col, node_pre, refined,
     part, part_in, col0, col1, choice, choice_in, own, csrc, cs_other, sb, outv,
     load_sem, label_sem, out_sem, halo_ss, halo_rs, part_ss, part_rs, ag_ss, ag_rs, set_ss, set_rs,
 ):
@@ -140,8 +140,9 @@
     src_col[...] = column_of(es[...])
     loads[0].wait()
     loads[1].wait()
-    a_own[...] = dot(states[...], wef[0, w : 2 * w]).astype(BF)
-    picked = dot(wanted, a_own[...]).astype(BF)
+    projected = dot(states[...], wef[0, w : 2 * w]).astype(BF)
+    picked = dot(wanted, projected).astype(BF)
+    wef[0, w : 2 * w] = projected
     pick[...] = picked.reshape(4, halo_rows, w)
     for copy in labels[3:]:
         copy.wait()
@@ -158,7 +159,7 @@
     cs_copy.start()
 
     loads[2].wait()
-    b_tgt[...] = dot(states[...], wef[0, 2 * w : 3 * w]).astype(BF)
+    wef[0, 2 * w : 3 * w] = dot(states[...], wef[0, 2 * w : 3 * w]).astype(BF)
     edges = lat.shape[0]
     loads[3].wait()
     loads[4].wait()
@@ -166,11 +167,9 @@
 
     def first(b, carry):
         here = pl.ds(pl.multiple_of(b * nodes, nodes), nodes)
-        pre[here, :] = (
-            dot(lat[here, :], wef[0, 0:w])
-            + dot(pick_matrix(src_col[here, :], nodes), a_own[...])
-            + dot(pick_matrix(tgt_col[here, :], nodes), b_tgt[...])
-        )
+        sources = pick_matrix(src_col[here, :], nodes)
+        targets = pick_matrix(tgt_col[here, :], nodes)
+        pre[here, :] = dot(jnp.concatenate([lat[here, :], sources, targets], axis=1), wef[0])
         return carry
 
     lax.fori_loop(0, blocks, first, 0, unroll=True)
@@ -433,8 +432,6 @@
         V((2, w, w), BF),
         V((w, w), BF),
         V((c_edges, w), BF),
-        V((nodes, w), BF),
-        V((nodes, w), BF),
         V((4, halo_rows, w), BF),
         V((4, halo_rows, w), BF),
         V((edges, w), F32),

time: 64.7 us -> 64.7 us (level)
  no operation moved by 1% of the time
where the time goes in v8:
time: 64.7 us; the launch traced here: 64.6 us
  Pallas kernels  62.1 us (96%)
  local copies, waits for them, and re-layouts  1.87 us (3%)
  between operations  0.66 us (1%)
    pallas_call x1, Pallas kernels, per_device(): pl.pallas_call(kernel, out_shape=jax.ShapeDtypeStruct((1, nodes, w), BF),...  62.1 us
    unnamed x1, local copies, waits for them, and re-layouts  1.87 us

profile of v8, /device:TPU:16, one launch (start us, length us, event | category | flops | bytes accessed | tf_op | source)
XLA Modules:
  0.0 64.6 jit_solution(16387162769163710009)
XLA Ops:
  0.7 62.1 %shard_map.163 = bf16[1,512,512]{2,1,0:T(8,128)(2,1)} custom-call(bf16[1,512,512]{2,1,0:T(8,128)(2,1)} %fn.1, bf16[1,2048,512]{2,1,0:T(8,128)(2,1)} %fe.1, s32[1,2048]{1,0:T(1,128)} %es_far.1, s32[1,2048]{1,0:T(1,128)} %et_far.1, s32[1,1]{1,0:T(1,128)S(6)} %copy.19.eb, s32[1,4,128]{2,1,0:T(4,128)} %sr_far.1, s32[1,512]{1,0:T(1,128)} %cm_far.1, ...), custom_call_target="tpu_custom_call" | custom-call | flops 8999999488 | bytes 12000000 | tf_op jit(solution)/shard_map/pallas_call | solution.py:465
  62.8 1.9 %copy.20 = bf16[1,512,512]{2,1,0:T(8,128)(2,1)} copy(bf16[1,512,512]{2,1,0:T(8,128)(2,1)} %shard_map.163) | data formatting | bytes 1048576
